TPU v7x, 256 devices: a whole 4x4x8 slice. The times are simulated.
256 devices in a mesh: vir: 32 (over x, z), occ: 8 (over y, core).
Axes of the slice: x: 4, y: 4, z: 8, core: 2. Of those that a mesh axis runs over, the one named last changes fastest.
Arguments:
- amplitudes: bfloat16 [65536, 6144], P('vir', 'occ'), may hold values from -6 to 6
- integrals: bfloat16 [8192, 128, 128], P(('vir', 'occ')), may hold values from -0.25 to 0.25
- task_block: int32 [8192], P('vir'), may hold values from 0 to 15
- task_source: int32 [8192], P('vir'), may hold values from 0 to 63
- task_count: int32 [32], P('vir'), may hold values from 128 to 256, as said below
Outputs:
- ladder: bfloat16 [65536, 6144], P('vir', 'occ')
Inputs may be any that keep to these rules, and one draw needn't show every extreme that they name: Vir index v's live tasks are its slots 0 to task_count[v] - 1; the other slots hold no task. Some vir index has all 256 slots live.
All inputs are finite; a program needn't handle non-finite values.
Results may differ from a plain program's by a relative error of at most 0.001.
Values may be sent and summed in bfloat16 or wider, within the bound.
A program may use at most 128 MiB of HBM per device.

v0:
```python
import jax
import jax.numpy as jnp
from jax import lax
from jax.sharding import PartitionSpec as P

GROUP = 4


batch_slots = 16


def partner_2(value, axis, stride):
    return lax.ppermute(value, axis, [(i, i ^ 1 << stride) for i in range(lax.axis_size(axis))])


def run_tasks(accumulated, tile_table, blocks, sources, live_count, group_rows):
    block_count = accumulated.shape[0]
    turn_count = (live_count + batch_slots - 1) // batch_slots

    def one_turn(turn_index, running):
        start = turn_index * batch_slots
        tile_part = lax.dynamic_slice_in_dim(tile_table, start, batch_slots, 0)
        block_part = lax.dynamic_slice_in_dim(blocks, start, batch_slots, 0)
        source_part = lax.dynamic_slice_in_dim(sources, start, batch_slots, 0)
        slot_ids = start + jnp.arange(batch_slots, dtype=jnp.int32)
        keep_mask = (slot_ids < live_count).astype(jnp.float32)
        chosen = jnp.take(group_rows, source_part, axis=0)
        partial_value = jnp.einsum(
            "kac,kcj->kaj", tile_part, chosen, preferred_element_type=jnp.float32
        )
        block_ids = jnp.arange(block_count, dtype=jnp.int32)
        one_hot = (block_part[:, None] == block_ids[None, :]).astype(jnp.float32) * keep_mask[
            :, None
        ]
        placed = jnp.einsum(
            "kb,kaj->baj",
            one_hot,
            partial_value,
            precision=lax.Precision.HIGHEST,
            preferred_element_type=jnp.float32,
        )
        return running + placed

    return lax.fori_loop(0, turn_count, one_turn, accumulated)


def local(amplitudes, integrals, task_block, task_source, task_count):
    tile_size = integrals.shape[1]
    pair_count = amplitudes.shape[1]
    block_count = amplitudes.shape[0] // tile_size
    tile_table = lax.all_gather(integrals, "occ", axis=0, tiled=True)
    position = lax.axis_index("vir")
    group_rows = amplitudes
    for bit_index in range(GROUP.bit_length() - 1):
        partner = partner_2(group_rows, "vir", bit_index)
        upper_half = position // 2**bit_index % 2
        group_rows = jnp.where(
            upper_half == 1,
            jnp.concatenate([partner, group_rows], 0),
            jnp.concatenate([group_rows, partner], 0),
        )
    group_rows = group_rows.reshape(GROUP * block_count, tile_size, pair_count)
    live_count = task_count[0]
    start_sum = jnp.zeros((block_count, tile_size, pair_count), jnp.float32)
    summed = run_tasks(start_sum, tile_table, task_block, task_source, live_count, group_rows)
    return summed.reshape(block_count * tile_size, pair_count).astype(jnp.bfloat16)


def solution(mesh):
    return jax.shard_map(
        local,
        mesh=mesh,
        in_specs=(P("vir", "occ"), P(("vir", "occ"), None, None), P("vir"), P("vir"), P("vir")),
        out_specs=P("vir", "occ"),
        check_vma=False,
    )
```

profile of v0, /device:TPU:82, one launch (start us, length us, event | category | flops | bytes accessed | tf_op | source)
XLA Modules:
  0.0 740.7 jit_solution(2463131990966863343)
XLA Ops:
  9.3 68.3 %collective-permute-done = bf16[2048,768]{1,0:T(8,128)(2,1)S(1)} collective-permute-done((bf16[2048,768]{1,0:T(8,128)(2,1)}, bf16[2048,768]{1,0:T(8,128)(2,1)S(1)}, u32[]{:S(2)}, u32[]{:S(2)}) %collective-permute-start) | collective-permute-done | bytes 3145760 | tf_op jit(solution)/shard_map/ppermute | solution.py:13
  77.6 7.3 maximum_select_fusion.1
  85.5 268.8 %collective-permute-done.1 = bf16[4096,768]{1,0:T(8,128)(2,1)} collective-permute-done((bf16[4096,768]{1,0:T(8,128)(2,1)}, bf16[4096,768]{1,0:T(8,128)(2,1)}, u32[]{:S(2)}, u32[]{:S(2)}) %collective-permute-start.1) | collective-permute-done | bytes 6291488 | tf_op jit(solution)/shard_map/ppermute | solution.py:13
  354.4 14.4 %maximum_select_fusion = bf16[8192,768]{1,0:T(8,128)(2,1)} fusion(bf16[4096,768]{1,0:T(8,128)(2,1)} %maximum_select_fusion.1, bf16[4096,768]{1,0:T(8,128)(2,1)} %collective-permute-done.1, pred[]{:T(512)S(6)} %eq.22), kind=kLoop, calls=%fused_computation.22 | loop fusion | flops 56623104 | bytes 25165824 | tf_op jit(solution)/shard_map/jit(_where)/select_n | solution.py:57
  372.3 355.7 %while.10 = (s32[]{:T(128)}, f32[16,128,768]{2,0,1:T(8,128)}, s32[]{:T(128)}, s32[256]{0:T(256)S(1)}, s32[]{:T(128)}, /*index=5*/bf16[256,128,128]{2,1,0:T(8,128...) while((s32[]{:T(128)}, f32[16,128,768]{2,0,1:T(8,128)}, ...), condition=%wide.region_1.2_spmd, body=%wide.region_0.1_spmd.sunk | while | flops 707790464 | bytes 85463888 | solution.py:44
  373.1 5.3 gather_fusion
  381.4 10.5 %fusion.29 = f32[16,128,768]{2,0,1:T(8,128)S(1)} fusion(f32[16,128,768]{2,0,1:T(8,128)S(1)} %copy-done, f32[16,128,768]{2,1,0:T(8,128)S(1)} %fusion.28, f32[16]{0:T(128)S(1)} %get-tuple-element.123, s32[16]{0:T(128)S(1)} %dynamic_slice.16), kind=kOutput, calls=%fused_computation.6.clone.1 | convolution fusion | flops 303563264 | bytes 18874496 | tf_op jit(solution)/shard_map/while/body/kb,kaj->baj/dot_general | solution.py:35
  395.3 5.3 gather_fusion
  403.6 10.5 %fusion.29 = f32[16,128,768]{2,0,1:T(8,128)S(1)} fusion(f32[16,128,768]{2,0,1:T(8,128)S(1)} %copy-done, f32[16,128,768]{2,1,0:T(8,128)S(1)} %fusion.28, f32[16]{0:T(128)S(1)} %get-tuple-element.123, s32[16]{0:T(128)S(1)} %dynamic_slice.16), kind=kOutput, calls=%fused_computation.6.clone.1 | convolution fusion | flops 303563264 | bytes 18874496 | tf_op jit(solution)/shard_map/while/body/kb,kaj->baj/dot_general | solution.py:35
  417.5 5.3 gather_fusion
  425.8 10.5 %fusion.29 = f32[16,128,768]{2,0,1:T(8,128)S(1)} fusion(f32[16,128,768]{2,0,1:T(8,128)S(1)} %copy-done, f32[16,128,768]{2,1,0:T(8,128)S(1)} %fusion.28, f32[16]{0:T(128)S(1)} %get-tuple-element.123, s32[16]{0:T(128)S(1)} %dynamic_slice.16), kind=kOutput, calls=%fused_computation.6.clone.1 | convolution fusion | flops 303563264 | bytes 18874496 | tf_op jit(solution)/shard_map/while/body/kb,kaj->baj/dot_general | solution.py:35
  448.1 10.5 %fusion.29 = f32[16,128,768]{2,0,1:T(8,128)S(1)} fusion(f32[16,128,768]{2,0,1:T(8,128)S(1)} %copy-done, f32[16,128,768]{2,1,0:T(8,128)S(1)} %fusion.28, f32[16]{0:T(128)S(1)} %get-tuple-element.123, s32[16]{0:T(128)S(1)} %dynamic_slice.16), kind=kOutput, calls=%fused_computation.6.clone.1 | convolution fusion | flops 303563264 | bytes 18874496 | tf_op jit(solution)/shard_map/while/body/kb,kaj->baj/dot_general | solution.py:35
  470.3 10.5 %fusion.29 = f32[16,128,768]{2,0,1:T(8,128)S(1)} fusion(f32[16,128,768]{2,0,1:T(8,128)S(1)} %copy-done, f32[16,128,768]{2,1,0:T(8,128)S(1)} %fusion.28, f32[16]{0:T(128)S(1)} %get-tuple-element.123, s32[16]{0:T(128)S(1)} %dynamic_slice.16), kind=kOutput, calls=%fused_computation.6.clone.1 | convolution fusion | flops 303563264 | bytes 18874496 | tf_op jit(solution)/shard_map/while/body/kb,kaj->baj/dot_general | solution.py:35
  492.5 10.5 %fusion.29 = f32[16,128,768]{2,0,1:T(8,128)S(1)} fusion(f32[16,128,768]{2,0,1:T(8,128)S(1)} %copy-done, f32[16,128,768]{2,1,0:T(8,128)S(1)} %fusion.28, f32[16]{0:T(128)S(1)} %get-tuple-element.123, s32[16]{0:T(128)S(1)} %dynamic_slice.16), kind=kOutput, calls=%fused_computation.6.clone.1 | convolution fusion | flops 303563264 | bytes 18874496 | tf_op jit(solution)/shard_map/while/body/kb,kaj->baj/dot_general | solution.py:35
  514.7 10.5 %fusion.29 = f32[16,128,768]{2,0,1:T(8,128)S(1)} fusion(f32[16,128,768]{2,0,1:T(8,128)S(1)} %copy-done, f32[16,128,768]{2,1,0:T(8,128)S(1)} %fusion.28, f32[16]{0:T(128)S(1)} %get-tuple-element.123, s32[16]{0:T(128)S(1)} %dynamic_slice.16), kind=kOutput, calls=%fused_computation.6.clone.1 | convolution fusion | flops 303563264 | bytes 18874496 | tf_op jit(solution)/shard_map/while/body/kb,kaj->baj/dot_general | solution.py:35
  537.0 10.5 %fusion.29 = f32[16,128,768]{2,0,1:T(8,128)S(1)} fusion(f32[16,128,768]{2,0,1:T(8,128)S(1)} %copy-done, f32[16,128,768]{2,1,0:T(8,128)S(1)} %fusion.28, f32[16]{0:T(128)S(1)} %get-tuple-element.123, s32[16]{0:T(128)S(1)} %dynamic_slice.16), kind=kOutput, calls=%fused_computation.6.clone.1 | convolution fusion | flops 303563264 | bytes 18874496 | tf_op jit(solution)/shard_map/while/body/kb,kaj->baj/dot_general | solution.py:35
  559.2 10.5 %fusion.29 = f32[16,128,768]{2,0,1:T(8,128)S(1)} fusion(f32[16,128,768]{2,0,1:T(8,128)S(1)} %copy-done, f32[16,128,768]{2,1,0:T(8,128)S(1)} %fusion.28, f32[16]{0:T(128)S(1)} %get-tuple-element.123, s32[16]{0:T(128)S(1)} %dynamic_slice.16), kind=kOutput, calls=%fused_computation.6.clone.1 | convolution fusion | flops 303563264 | bytes 18874496 | tf_op jit(solution)/shard_map/while/body/kb,kaj->baj/dot_general | solution.py:35
  581.4 10.5 %fusion.29 = f32[16,128,768]{2,0,1:T(8,128)S(1)} fusion(f32[16,128,768]{2,0,1:T(8,128)S(1)} %copy-done, f32[16,128,768]{2,1,0:T(8,128)S(1)} %fusion.28, f32[16]{0:T(128)S(1)} %get-tuple-element.123, s32[16]{0:T(128)S(1)} %dynamic_slice.16), kind=kOutput, calls=%fused_computation.6.clone.1 | convolution fusion | flops 303563264 | bytes 18874496 | tf_op jit(solution)/shard_map/while/body/kb,kaj->baj/dot_general | solution.py:35
  603.7 10.5 %fusion.29 = f32[16,128,768]{2,0,1:T(8,128)S(1)} fusion(f32[16,128,768]{2,0,1:T(8,128)S(1)} %copy-done, f32[16,128,768]{2,1,0:T(8,128)S(1)} %fusion.28, f32[16]{0:T(128)S(1)} %get-tuple-element.123, s32[16]{0:T(128)S(1)} %dynamic_slice.16), kind=kOutput, calls=%fused_computation.6.clone.1 | convolution fusion | flops 303563264 | bytes 18874496 | tf_op jit(solution)/shard_map/while/body/kb,kaj->baj/dot_general | solution.py:35
  625.9 10.5 %fusion.29 = f32[16,128,768]{2,0,1:T(8,128)S(1)} fusion(f32[16,128,768]{2,0,1:T(8,128)S(1)} %copy-done, f32[16,128,768]{2,1,0:T(8,128)S(1)} %fusion.28, f32[16]{0:T(128)S(1)} %get-tuple-element.123, s32[16]{0:T(128)S(1)} %dynamic_slice.16), kind=kOutput, calls=%fused_computation.6.clone.1 | convolution fusion | flops 303563264 | bytes 18874496 | tf_op jit(solution)/shard_map/while/body/kb,kaj->baj/dot_general | solution.py:35
  648.1 10.5 %fusion.29 = f32[16,128,768]{2,0,1:T(8,128)S(1)} fusion(f32[16,128,768]{2,0,1:T(8,128)S(1)} %copy-done, f32[16,128,768]{2,1,0:T(8,128)S(1)} %fusion.28, f32[16]{0:T(128)S(1)} %get-tuple-element.123, s32[16]{0:T(128)S(1)} %dynamic_slice.16), kind=kOutput, calls=%fused_computation.6.clone.1 | convolution fusion | flops 303563264 | bytes 18874496 | tf_op jit(solution)/shard_map/while/body/kb,kaj->baj/dot_general | solution.py:35
  670.4 10.5 %fusion.29 = f32[16,128,768]{2,0,1:T(8,128)S(1)} fusion(f32[16,128,768]{2,0,1:T(8,128)S(1)} %copy-done, f32[16,128,768]{2,1,0:T(8,128)S(1)} %fusion.28, f32[16]{0:T(128)S(1)} %get-tuple-element.123, s32[16]{0:T(128)S(1)} %dynamic_slice.16), kind=kOutput, calls=%fused_computation.6.clone.1 | convolution fusion | flops 303563264 | bytes 18874496 | tf_op jit(solution)/shard_map/while/body/kb,kaj->baj/dot_general | solution.py:35
  692.6 10.5 %fusion.29 = f32[16,128,768]{2,0,1:T(8,128)S(1)} fusion(f32[16,128,768]{2,0,1:T(8,128)S(1)} %copy-done, f32[16,128,768]{2,1,0:T(8,128)S(1)} %fusion.28, f32[16]{0:T(128)S(1)} %get-tuple-element.123, s32[16]{0:T(128)S(1)} %dynamic_slice.16), kind=kOutput, calls=%fused_computation.6.clone.1 | convolution fusion | flops 303563264 | bytes 18874496 | tf_op jit(solution)/shard_map/while/body/kb,kaj->baj/dot_general | solution.py:35
  714.8 10.5 %fusion.29 = f32[16,128,768]{2,0,1:T(8,128)S(1)} fusion(f32[16,128,768]{2,0,1:T(8,128)S(1)} %copy-done, f32[16,128,768]{2,1,0:T(8,128)S(1)} %fusion.28, f32[16]{0:T(128)S(1)} %get-tuple-element.123, s32[16]{0:T(128)S(1)} %dynamic_slice.16), kind=kOutput, calls=%fused_computation.6.clone.1 | convolution fusion | flops 303563264 | bytes 18874496 | tf_op jit(solution)/shard_map/while/body/kb,kaj->baj/dot_general | solution.py:35
  (153 shorter events, 183.2 us)
Async XLA Ops:
  6.5 362.3 %all-gather.2.cloned.1.call-start = ((), (), s32[]{:S(2)}) async-start(), calls=%async_computation | async-start | bytes 9437184 | tf_op jit(solution)/shard_map/all_gather | solution.py:51
  7.3 70.3 %collective-permute-start = (bf16[2048,768]{1,0:T(8,128)(2,1)}, bf16[2048,768]{1,0:T(8,128)(2,1)S(1)}, u32[]{:S(2)}, u32[]{:S(2)}) collective-permute-start(bf16[2048,768]{1,0:T(8,128)(2,1)} %param.7), channel_id=1, source_target_pairs={{0,8},{8,0},{16,24},{24,16},{32,40},{40,32},{48,56},{56,48},{64,72... | collective-permute-start | bytes 9437192 | tf_op jit(solution)/shard_map/ppermute | solution.py:13
  84.9 269.5 %collective-permute-start.1 = (bf16[4096,768]{1,0:T(8,128)(2,1)}, bf16[4096,768]{1,0:T(8,128)(2,1)}, u32[]{:S(2)}, u32[]{:S(2)}) collective-permute-start(bf16[4096,768]{1,0:T(8,128)(2,1)} %maximum_select_fusion.1), channel_id=1, source_target_pairs={{0,16},{8,24},{16,0},{24,8},{32,48},{40,56},{48,32},{56,40},{64,80... | collective-permute-start | bytes 18874376 | tf_op jit(solution)/shard_map/ppermute | solution.py:13
  368.8 3.5 copy-start.2
  368.8 3.5 copy-start.3
  378.4 2.9 copy-start
  400.6 2.9 copy-start
  414.1 2.6 copy-start.1
  422.9 2.9 copy-start
  445.1 2.9 copy-start
  467.3 2.9 copy-start
  489.6 2.9 copy-start
  511.8 2.9 copy-start
  534.0 2.9 copy-start
  556.3 2.9 copy-start
  578.5 2.9 copy-start
  600.7 2.9 copy-start
  623.0 2.9 copy-start
  636.4 2.6 copy-start.1
  645.2 2.9 copy-start
  658.6 2.6 copy-start.1
  667.4 2.9 copy-start
  689.7 2.9 copy-start
  711.9 2.9 copy-start
  (13 other events, 34.4 us)
Sparse Core Ops, SparseCore 0:
  9.2 53.2 all-gather.1
where the time goes:
time: 742 us; the launch traced here: 741 us
  waiting for transfers between devices  338 us (46%)
  matrix products  204 us (27%)
  local copies, waits for them, and re-layouts  146 us (20%)
  other arithmetic  36.6 us (5%)
  between operations  14.1 us (2%)
    ppermute x2, waiting for transfers between devices, partner_2(): lax.ppermute(value, axis, [(i, i ^ 1 << stride) for i in range(lax.axis_s...  337 us
    dot_general x16, matrix products, one_turn(): jnp.einsum('kb,kaj->baj', one_hot, partial_value, precision=lax.Precision...  168 us
    gather x16, local copies, waits for them, and re-layouts, one_turn(): chosen = jnp.take(group_rows, source_part, axis=0)  85.2 us
    while x64, local copies, waits for them, and re-layouts  53.3 us
    dot_general x16, matrix products, one_turn(): jnp.einsum('kac,kcj->kaj', tile_part, chosen, preferred_element_type=jnp....  35.8 us
    select_n x2, other arithmetic, local(): jnp.where(upper_half == 1, jnp.concatenate([partner, group_rows], 0), jnp...  21.7 us
  transfers between devices with their start and end apart: 3, of which 2 were waited for; matrix products, arithmetic and copies ran while one was open for 3% of the time, Pallas kernels for 0%

commit v1 on v0

v1 whole, which is shorter than its diff:
```python
import functools

import jax
import jax.numpy as jnp
from jax import lax
from jax.sharding import PartitionSpec as P
import jax.experimental.pallas as pl
import jax.experimental.pallas.tpu as pltpu

MESH = pl.DeviceIdType.MESH
ZLEN = 8
GROUP = 4
YLEN = 4
TILE = 128
BLOCKS = 16
SLOTS = 256
SHARD = 32
PAIRS = (SLOTS + BLOCKS) // 2
ROW = 384
WIDTHS = (128, 128, 256, 128, 128)
STARTS = (0, 128, 256, 512, 640)
N = len(WIDTHS)
UNROLL = 8


def task_table(count, block, source):
    i32 = jnp.int32
    slot_l = lax.broadcasted_iota(i32, (SLOTS, SLOTS), 1)
    slot_s = lax.broadcasted_iota(i32, (SLOTS, SLOTS), 0)
    key_l = jnp.where(slot_l < count, jnp.broadcast_to(block, (SLOTS, SLOTS)), BLOCKS)
    key_s = key_l.T
    source_s = jnp.broadcast_to(source, (SLOTS, SLOTS)).T[:, 0:1]
    before = jnp.where((key_l == key_s) & (slot_l < slot_s), 1, 0)
    order = jnp.sum(before, axis=1, keepdims=True)
    key = key_s[:, 0:1]
    blk_s = lax.broadcasted_iota(i32, (BLOCKS, SLOTS), 0)
    n_s = jnp.sum(jnp.where(key_l[0:BLOCKS] == blk_s, 1, 0), axis=1, keepdims=True)
    even_s = ((n_s + 1) // 2) * 2
    lane = lax.broadcasted_iota(i32, (SLOTS, ROW), 1)
    n_l = jnp.sum(jnp.where(key == lane, 1, 0), axis=0, keepdims=True)
    n_l = jnp.where(lane[0:1] < BLOCKS, n_l, 0)
    even_l = ((n_l + 1) // 2) * 2
    lane16 = lax.broadcasted_iota(i32, (BLOCKS, ROW), 1)
    sub16 = lax.broadcasted_iota(i32, (BLOCKS, ROW), 0)
    base_l = jnp.sum(jnp.where(sub16 < lane16, even_s, 0), axis=0, keepdims=True)
    base_s = jnp.sum(jnp.where(lane16 < sub16, even_l, 0), axis=1, keepdims=True)
    base = jnp.sum(jnp.where(lane < key, even_l, 0), axis=1, keepdims=True)
    place = jnp.where(key < BLOCKS, base + order, ROW)
    here = place == lane
    slot = lax.broadcasted_iota(i32, (SLOTS, ROW), 0)
    amp = jnp.sum(jnp.where(here, source_s, 0), axis=0, keepdims=True)
    integral = SLOTS + jnp.sum(jnp.where(here, slot - SLOTS, 0), axis=0, keepdims=True)
    begins = jnp.where((base_s == 2 * lane16) & (n_s > 0), 1, 0)
    goes_on = 1 - jnp.sum(begins, axis=0, keepdims=True)
    last = jnp.maximum((base_l + even_l) // 2 - 1, 0)
    last = jnp.where(lane[0:1] < BLOCKS, last, 0)
    filled = jnp.where(n_l > 0, 1, 0)
    row = lax.broadcasted_iota(i32, (8, ROW), 0)
    out = jnp.where(row == 0, amp, 0)
    for k, value in ((1, integral), (2, goes_on), (3, last), (4, filled)):
        out = jnp.where(row == k, value, out)
    return out


def kernel(amp_ref, int_ref, block_ref, source_ref, count_ref, out_ref, *scratch):
    held = scratch[0:N]
    done = scratch[N : 2 * N]
    mine = scratch[2 * N : 3 * N]
    (tiles_own, tiles_out, prefix, table_own, table_out, smem_own, smem_out,
     s_own, r_own, s_fwd, r_fwd, s_amp, r_amp, s_res, r_res, l_amp, l_out,
     s_ring, r_ring, s_half, r_half, s_core, r_core, s_v, r_v, s_tab, r_tab,
     l_v, l_tab) = scratch[3 * N :]
    tiles = (tiles_own, tiles_out)

    vir = lax.axis_index("vir")
    occ = lax.axis_index("occ")
    pos = vir % GROUP
    first = vir - pos
    y, core = occ // 2, occ % 2
    inner = (pos == 1) | (pos == 2)
    partner_pos = jnp.where(pos < 2, 1 - pos, 5 - pos)
    partner = (first + partner_pos, occ)
    cross_pos = 3 - pos
    cross = (first + cross_pos, occ)
    cross_partner_pos = jnp.where(cross_pos < 2, 1 - cross_pos, 5 - cross_pos)
    y_up = (vir, ((y + 1) % YLEN) * 2 + core)
    y_down = (vir, ((y + 3) % YLEN) * 2 + core)
    other = (vir, y * 2 + 1 - core)

    def part(ref, where):
        return ref.at[pl.ds(where * BLOCKS, BLOCKS)]

    def shard(p, yy, cc, begin=0, size=SHARD):
        start = ((yy % YLEN) * 2 + cc) * SHARD + begin
        return tiles[p].at[pl.ds(start, size)]

    def columns(ref, c):
        return ref.at[:, :, pl.ds(STARTS[c], WIDTHS[c])]

    def send(src, dst, ssem, rsem, to):
        return pltpu.make_async_remote_copy(
            src_ref=src, dst_ref=dst, send_sem=ssem, recv_sem=rsem, device_id=to, device_id_type=MESH
        )

    barrier = pltpu.get_barrier_semaphore()

    def load_amp(c):
        return pltpu.make_async_copy(columns(amp_ref, c), part(held[c], pos), l_amp.at[c])

    def amp_in(c, where):
        return send(part(held[c], where), part(held[c], where), s_amp.at[c], r_amp.at[c], partner)

    def v_in():
        return send(int_ref, shard(1, y, core), s_v, r_v, partner)

    def tab_in():
        return send(table_own, table_out, s_tab, r_tab, partner)

    def result(c, where):
        return send(done[c], part(held[c], where), s_res.at[c], r_res.at[c], partner)

    @pl.when(jnp.logical_not(inner))
    def _():
        pl.semaphore_signal(barrier, inc=1, device_id=partner, device_id_type=MESH)
        for c in range(N):
            load_amp(c).start()
        table_own[...] = task_table(count_ref[0], block_ref[...], source_ref[...])
        pl.semaphore_wait(barrier, 1)
        tab_in().start()
        v_in().start()
        queue = [v_in()]
        for c in range(N):
            load_amp(c).wait()
            if len(queue) > 1:
                queue.pop(0).wait_send()
            copy = amp_in(c, pos)
            copy.start()
            queue.append(copy)
        for copy in queue:
            copy.wait_send()
        tab_in().wait_send()
        for c in range(N):
            result(c, partner_pos).wait_recv()
            pltpu.make_async_copy(part(held[c], partner_pos), columns(out_ref, c), l_out.at[c]).start()
        for c in range(N):
            pltpu.make_async_copy(part(held[c], partner_pos), columns(out_ref, c), l_out.at[c]).wait()

    @pl.when(inner)
    def _():
        for to in (partner, cross, y_up, y_down, other):
            pl.semaphore_signal(barrier, inc=1, device_id=to, device_id_type=MESH)
        for c in range(N):
            load_amp(c).start()
        load_v = pltpu.make_async_copy(int_ref, shard(0, y, core), l_v)
        load_v.start()
        pl.semaphore_wait(barrier, 5)

        def own(c):
            return send(part(held[c], pos), part(held[c], pos), s_own.at[c], r_own.at[c], cross)

        def own_in(c):
            return send(part(held[c], pos), part(held[c], cross_pos), s_own.at[c], r_own.at[c], cross)

        def fwd(c):
            return send(part(held[c], partner_pos), part(held[c], partner_pos), s_fwd.at[c], r_fwd.at[c], cross)

        def fwd_in(c):
            return send(part(held[c], partner_pos), part(held[c], cross_partner_pos), s_fwd.at[c], r_fwd.at[c], cross)

        def ring(p, way, src=None):
            src = shard(p, y, core) if src is None else src
            return send(src, shard(p, y, core), s_ring.at[p, way], r_ring.at[p, way], (y_up, y_down)[way])

        def ring_in(p, way):
            return send(shard(p, y, core), shard(p, y + (3, 1)[way], core), s_ring.at[p, way], r_ring.at[p, way],
                        (y_up, y_down)[way])

        def half(p, way):
            ref = shard(p, y + (3, 1)[way], core, way * (SHARD // 2), SHARD // 2)
            return send(ref, ref, s_half.at[p, way], r_half.at[p, way], (y_up, y_down)[way])

        def half_in(p, way):
            ref = shard(p, y + 2, core, way * (SHARD // 2), SHARD // 2)
            return send(ref, ref, s_half.at[p, way], r_half.at[p, way], (y_up, y_down)[way])

        def swap(p, turn, src=None):
            ref = shard(p, y + turn, core)
            return send(ref if src is None else src, ref, s_core.at[p, turn], r_core.at[p, turn], other)

        def swap_in(p, turn):
            return send(shard(p, y + turn, core), shard(p, y + turn, 1 - core), s_core.at[p, turn],
                        r_core.at[p, turn], other)

        def ring_on(p):
            for way in range(2):
                ring_in(p, way).wait_recv()
                half(p, way).start()
                swap(p, (3, 1)[way]).start()

        def ring_end(p):
            for way in range(2):
                half_in(p, way).wait_recv()
            swap(p, 2).start()
            for turn in range(YLEN):
                swap_in(p, turn).wait_recv()

        load_amp(0).wait()
        own(0).start()
        ring(0, 0, int_ref).start()
        ring(0, 1, int_ref).start()
        load_amp(1).wait()
        own(1).start()
        load_amp(2).wait()
        own(2).start()
        swap(0, 0, int_ref).start()

        tiles_own[SLOTS] = jnp.zeros((TILE, TILE), jnp.bfloat16)
        tiles_out[SLOTS] = jnp.zeros((TILE, TILE), jnp.bfloat16)
        table_own[...] = task_table(count_ref[0], block_ref[...], source_ref[...])
        tab_a = pltpu.make_async_copy(table_own, smem_own, l_tab.at[0])
        tab_a.start()
        tab_in().wait_recv()
        tab_b = pltpu.make_async_copy(table_out, smem_out, l_tab.at[1])
        tab_b.start()
        load_v.wait()
        tab_a.wait()
        tab_b.wait()
        for c in range(3, N):
            load_amp(c).wait()

        def compute(c, p):
            width = WIDTHS[c]
            smem = (smem_own, smem_out)[p]
            target = (mine, done)[p][c]

            def pair(j, total):
                a, b = 2 * j, 2 * j + 1
                left = jnp.concatenate([tiles[p][smem[1, a]], tiles[p][smem[1, b]]], 1)
                right = jnp.concatenate([held[c][smem[0, a]], held[c][smem[0, b]]], 0)
                product = jnp.dot(left, right, preferred_element_type=jnp.float32)
                total = total * smem[2, j].astype(jnp.float32) + product
                prefix[j, :, 0:width] = total.astype(jnp.bfloat16)
                return total

            lax.fori_loop(0, PAIRS, pair, jnp.zeros((TILE, width), jnp.float32), unroll=UNROLL)

            def place(b, carry):
                value = prefix[smem[3, b], :, 0:width].astype(jnp.float32)
                target[b] = (value * smem[4, b].astype(jnp.float32)).astype(jnp.bfloat16)
                return carry

            lax.fori_loop(0, BLOCKS, place, 0)
            if p:
                result(c, pos).start()
            else:
                pltpu.make_async_copy(target, columns(out_ref, c), l_out.at[c]).start()

        def issue_fwd(c):
            amp_in(c, partner_pos).wait_recv()
            fwd(c).start()

        def chunk_in(c):
            own_in(c).wait_recv()
            fwd_in(c).wait_recv()

        ring_on(0)
        v_in().wait_recv()
        ring(1, 0).start()
        ring(1, 1).start()
        swap(1, 0).start()
        own(0).wait_send()
        issue_fwd(0)
        own(1).wait_send()
        issue_fwd(1)
        ring_end(0)
        own(2).wait_send()
        issue_fwd(2)
        ring_on(1)
        chunk_in(0)
        compute(0, 0)
        fwd(0).wait_send()
        own(3).start()
        ring_end(1)
        compute(0, 1)
        chunk_in(1)
        compute(1, 1)
        fwd(1).wait_send()
        issue_fwd(3)
        compute(1, 0)
        fwd(2).wait_send()
        own(4).start()
        chunk_in(2)
        compute(2, 1)
        own(3).wait_send()
        issue_fwd(4)
        compute(2, 0)
        chunk_in(3)
        compute(3, 1)
        compute(3, 0)
        chunk_in(4)
        compute(4, 1)
        compute(4, 0)

        fwd(3).wait_send()
        own(4).wait_send()
        fwd(4).wait_send()
        for p in range(2):
            for way in range(2):
                ring(p, way).wait_send()
                half(p, way).wait_send()
            for turn in range(YLEN):
                swap(p, turn).wait_send()
        for c in range(N):
            result(c, pos).wait_send()
            pltpu.make_async_copy(mine[c], columns(out_ref, c), l_out.at[c]).wait()


def local(amplitudes, integrals, task_block, task_source, task_count):
    pair_count = amplitudes.shape[1]
    dma = pltpu.SemaphoreType.DMA
    bf16 = jnp.bfloat16
    chunks = [pltpu.VMEM((BLOCKS, TILE, w), bf16) for w in WIDTHS]
    scratch = [pltpu.VMEM((GROUP * BLOCKS, TILE, w), bf16) for w in WIDTHS] + chunks + chunks
    scratch += [
        pltpu.VMEM((SLOTS + 1, TILE, TILE), bf16),
        pltpu.VMEM((SLOTS + 1, TILE, TILE), bf16),
        pltpu.VMEM((PAIRS, TILE, max(WIDTHS)), bf16),
        pltpu.VMEM((8, ROW), jnp.int32),
        pltpu.VMEM((8, ROW), jnp.int32),
        pltpu.SMEM((8, ROW), jnp.int32),
        pltpu.SMEM((8, ROW), jnp.int32),
    ]
    scratch += [dma((N,))] * 10
    scratch += [dma((2, 2))] * 4 + [dma((2, YLEN))] * 2 + [dma] * 5 + [dma((2,))]
    any_space = pl.BlockSpec(memory_space=pl.ANY)
    vmem = pl.BlockSpec(memory_space=pltpu.VMEM)
    smem = pl.BlockSpec(memory_space=pltpu.SMEM)
    result = pl.pallas_call(
        kernel,
        name="ladder",
        out_shape=jax.ShapeDtypeStruct((BLOCKS, TILE, pair_count), bf16),
        in_specs=[any_space, any_space, vmem, vmem, smem],
        out_specs=any_space,
        scratch_shapes=scratch,
        compiler_params=pltpu.CompilerParams(
            collective_id=0, has_side_effects=True, vmem_limit_bytes=60 * 2**20
        ),
        cost_estimate=pl.CostEstimate(
            flops=4 * SLOTS * TILE * TILE * pair_count, bytes_accessed=8 * 2**20, transcendentals=0
        ),
    )(
        amplitudes.reshape(BLOCKS, TILE, pair_count),
        integrals,
        task_block.reshape(1, SLOTS),
        task_source.reshape(1, SLOTS),
        task_count,
    )
    return result.reshape(BLOCKS * TILE, pair_count)


def solution(mesh):
    return jax.shard_map(
        local,
        mesh=mesh,
        in_specs=(P("vir", "occ"), P(("vir", "occ"), None, None), P("vir"), P("vir"), P("vir")),
        out_specs=P("vir", "occ"),
        check_vma=False,
    )
```

time: 742 us -> 169 us (0.23)
  the two profiles are of different devices: /device:TPU:82 before, /device:TPU:1 now
where the time goes in v1:
time: 169 us; the launch traced here: 168 us
  Pallas kernels  164 us (97%)
  local copies, waits for them, and re-layouts  3.76 us (2%)
    pallas_call x1, Pallas kernels, local(): pl.pallas_call(kernel, name='ladder', out_shape=jax.ShapeDtypeStruct((BLO...  164 us
    unnamed x1, local copies, waits for them, and re-layouts  3.76 us

profile of v1, /device:TPU:1, one launch (start us, length us, event | category | flops | bytes accessed | tf_op | source)
XLA Modules:
  0.0 168.4 jit_solution(10074495641114238383)
XLA Ops:
  0.7 164.0 %ladder.1 = bf16[16,128,768]{2,1,0:T(8,128)(2,1)} custom-call(bf16[16,128,768]{2,1,0:T(8,128)(2,1)} %bitcast.5, bf16[32,128,128]{2,1,0:T(8,128)(2,1)} %int_ref.1, s32[1,256]{1,0:T(1,128)} %bitcast.6, s32[1,256]{1,0:T(1,128)} %bitcast.7, s32[1]{0:T(128)S(6)} %copy.7.count_ref), custom_call_target="tpu_custom_call" | custom-call | flops 12884901888 | bytes 8388608 | tf_op jit(solution)/shard_map/ladder/pallas_call | solution.py:338
  164.6 3.8 %copy.8 = bf16[2048,768]{1,0:T(8,128)(2,1)} copy(bf16[2048,768]{1,0:T(8,128)(2,1)} %bitcast.4) | data formatting | bytes 6291456

commit v2 on v1

--- a/solution.py
+++ b/solution.py
@@ -12,15 +12,17 @@
 GROUP = 4
 YLEN = 4
 TILE = 128
+HALF = TILE // 2
 BLOCKS = 16
 SLOTS = 256
 SHARD = 32
 PAIRS = (SLOTS + BLOCKS) // 2
 ROW = 384
-WIDTHS = (128, 128, 256, 128, 128)
-STARTS = (0, 128, 256, 512, 640)
+WIDTHS = (128,) * 6
+STARTS = (0, 128, 256, 384, 512, 640)
 N = len(WIDTHS)
-UNROLL = 8
+UNROLL = 17
+UNROLL_LAST = 34
 
 
 def task_table(count, block, source):
@@ -62,14 +64,14 @@
     return out
 
 
-def kernel(amp_ref, int_ref, block_ref, source_ref, count_ref, out_ref, *scratch):
+def kernel(amp_ref, int_ref, block_hbm, source_hbm, count_ref, out_ref, *scratch):
     held = scratch[0:N]
     done = scratch[N : 2 * N]
     mine = scratch[2 * N : 3 * N]
     (tiles_own, tiles_out, prefix, table_own, table_out, smem_own, smem_out,
      s_own, r_own, s_fwd, r_fwd, s_amp, r_amp, s_res, r_res, l_amp, l_out,
      s_ring, r_ring, s_half, r_half, s_core, r_core, s_v, r_v, s_tab, r_tab,
-     l_v, l_tab) = scratch[3 * N :]
+     l_v, l_tab, turn_sem, block_ref, source_ref, l_list, s_part, r_part) = scratch[3 * N :]
     tiles = (tiles_own, tiles_out)
 
     vir = lax.axis_index("vir")
@@ -103,6 +105,15 @@
         )
 
     barrier = pltpu.get_barrier_semaphore()
+    lists = [
+        pltpu.make_async_copy(block_hbm, block_ref, l_list.at[0]),
+        pltpu.make_async_copy(source_hbm, source_ref, l_list.at[1]),
+    ]
+
+    def make_table():
+        for copy in lists:
+            copy.wait()
+        table_own[...] = task_table(count_ref[0], block_ref[...], source_ref[...])
 
     def load_amp(c):
         return pltpu.make_async_copy(columns(amp_ref, c), part(held[c], pos), l_amp.at[c])
@@ -116,19 +127,27 @@
     def tab_in():
         return send(table_own, table_out, s_tab, r_tab, partner)
 
-    def result(c, where):
-        return send(done[c], part(held[c], where), s_res.at[c], r_res.at[c], partner)
+    def result(c):
+        return send(done[c], columns(out_ref, c), s_res.at[c], r_res.at[c], partner)
+
+    def result_part(c, top, rows):
+        k = top // rows
+        return send(done[c].at[:, pl.ds(top, rows)], columns(out_ref, c).at[:, pl.ds(top, rows)],
+                    s_part.at[k], r_part.at[k], partner)
 
     @pl.when(jnp.logical_not(inner))
     def _():
         pl.semaphore_signal(barrier, inc=1, device_id=partner, device_id_type=MESH)
         for c in range(N):
             load_amp(c).start()
-        table_own[...] = task_table(count_ref[0], block_ref[...], source_ref[...])
+        for copy in lists:
+            copy.start()
         pl.semaphore_wait(barrier, 1)
+        v_in().start()
+        make_table()
         tab_in().start()
-        v_in().start()
-        queue = [v_in()]
+        v_in().wait_send()
+        queue = []
         for c in range(N):
             load_amp(c).wait()
             if len(queue) > 1:
@@ -139,11 +158,10 @@
         for copy in queue:
             copy.wait_send()
         tab_in().wait_send()
-        for c in range(N):
-            result(c, partner_pos).wait_recv()
-            pltpu.make_async_copy(part(held[c], partner_pos), columns(out_ref, c), l_out.at[c]).start()
-        for c in range(N):
-            pltpu.make_async_copy(part(held[c], partner_pos), columns(out_ref, c), l_out.at[c]).wait()
+        for c in range(N - 1):
+            result(c).wait_recv()
+        for k in range(2):
+            result_part(N - 1, k * HALF, HALF).wait_recv()
 
     @pl.when(inner)
     def _():
@@ -153,6 +171,8 @@
             load_amp(c).start()
         load_v = pltpu.make_async_copy(int_ref, shard(0, y, core), l_v)
         load_v.start()
+        for copy in lists:
+            copy.start()
         pl.semaphore_wait(barrier, 5)
 
         def own(c):
@@ -191,16 +211,21 @@
             return send(shard(p, y + turn, core), shard(p, y + turn, 1 - core), s_core.at[p, turn],
                         r_core.at[p, turn], other)
 
+        def ring_come(p):
+            for way in range(2):
+                ring_in(p, way).wait_recv()
+                swap(p, (3, 1)[way]).start()
+
         def ring_on(p):
             for way in range(2):
-                ring_in(p, way).wait_recv()
                 half(p, way).start()
-                swap(p, (3, 1)[way]).start()
 
         def ring_end(p):
             for way in range(2):
                 half_in(p, way).wait_recv()
             swap(p, 2).start()
+
+        def swap_end(p):
             for turn in range(YLEN):
                 swap_in(p, turn).wait_recv()
 
@@ -210,13 +235,13 @@
         ring(0, 1, int_ref).start()
         load_amp(1).wait()
         own(1).start()
+        swap(0, 0, int_ref).start()
         load_amp(2).wait()
         own(2).start()
-        swap(0, 0, int_ref).start()
 
         tiles_own[SLOTS] = jnp.zeros((TILE, TILE), jnp.bfloat16)
         tiles_out[SLOTS] = jnp.zeros((TILE, TILE), jnp.bfloat16)
-        table_own[...] = task_table(count_ref[0], block_ref[...], source_ref[...])
+        make_table()
         tab_a = pltpu.make_async_copy(table_own, smem_own, l_tab.at[0])
         tab_a.start()
         tab_in().wait_recv()
@@ -228,30 +253,34 @@
         for c in range(3, N):
             load_amp(c).wait()
 
-        def compute(c, p):
+        def compute(c, p, top=0, rows=TILE):
             width = WIDTHS[c]
             smem = (smem_own, smem_out)[p]
             target = (mine, done)[p][c]
 
             def pair(j, total):
                 a, b = 2 * j, 2 * j + 1
-                left = jnp.concatenate([tiles[p][smem[1, a]], tiles[p][smem[1, b]]], 1)
+                left = jnp.concatenate(
+                    [tiles[p][smem[1, a], top : top + rows], tiles[p][smem[1, b], top : top + rows]], 1
+                )
                 right = jnp.concatenate([held[c][smem[0, a]], held[c][smem[0, b]]], 0)
                 product = jnp.dot(left, right, preferred_element_type=jnp.float32)
                 total = total * smem[2, j].astype(jnp.float32) + product
-                prefix[j, :, 0:width] = total.astype(jnp.bfloat16)
+                prefix[j, 0:rows, 0:width] = total.astype(jnp.bfloat16)
                 return total
 
-            lax.fori_loop(0, PAIRS, pair, jnp.zeros((TILE, width), jnp.float32), unroll=UNROLL)
+            lax.fori_loop(0, PAIRS, pair, jnp.zeros((rows, width), jnp.float32), unroll=UNROLL_LAST if (c, p) == (N - 1, 1) else UNROLL)
 
             def place(b, carry):
-                value = prefix[smem[3, b], :, 0:width].astype(jnp.float32)
-                target[b] = (value * smem[4, b].astype(jnp.float32)).astype(jnp.bfloat16)
+                value = prefix[smem[3, b], 0:rows, 0:width].astype(jnp.float32)
+                target[b, top : top + rows] = (value * smem[4, b].astype(jnp.float32)).astype(jnp.bfloat16)
                 return carry
 
             lax.fori_loop(0, BLOCKS, place, 0)
-            if p:
-                result(c, pos).start()
+            if p and rows < TILE:
+                result_part(c, top, rows).start()
+            elif p:
+                result(c).start()
             else:
                 pltpu.make_async_copy(target, columns(out_ref, c), l_out.at[c]).start()
 
@@ -263,47 +292,86 @@
             own_in(c).wait_recv()
             fwd_in(c).wait_recv()
 
-        ring_on(0)
+        ring_come(0)
         v_in().wait_recv()
         ring(1, 0).start()
         ring(1, 1).start()
         swap(1, 0).start()
         own(0).wait_send()
+        own(3).start()
+        own(1).wait_send()
         issue_fwd(0)
-        own(1).wait_send()
+        ring_come(1)
+        ring_on(1)
+        own(2).wait_send()
         issue_fwd(1)
+        ring_end(1)
+        ring_on(0)
+        own(3).wait_send()
+        issue_fwd(2)
+        swap_end(1)
+        chunk_in(0)
+        compute(0, 1)
         ring_end(0)
-        own(2).wait_send()
-        issue_fwd(2)
-        ring_on(1)
-        chunk_in(0)
-        compute(0, 0)
         fwd(0).wait_send()
-        own(3).start()
-        ring_end(1)
-        compute(0, 1)
+        issue_fwd(3)
+        swap_end(0)
         chunk_in(1)
         compute(1, 1)
+        compute(0, 0)
         fwd(1).wait_send()
-        issue_fwd(3)
-        compute(1, 0)
-        fwd(2).wait_send()
         own(4).start()
         chunk_in(2)
         compute(2, 1)
-        own(3).wait_send()
+        compute(1, 0)
+        fwd(2).wait_send()
         issue_fwd(4)
-        compute(2, 0)
         chunk_in(3)
         compute(3, 1)
+        compute(2, 0)
+        fwd(3).wait_send()
+
+        @pl.when(core == 0)
+        def _():
+            own(5).start()
+
         compute(3, 0)
+        own(4).wait_send()
+
+        @pl.when(core == 0)
+        def _():
+            issue_fwd(5)
+
         chunk_in(4)
+
+        @pl.when(core == 0)
+        def _():
+            own(5).wait_send()
+            pl.semaphore_signal(turn_sem, inc=1, device_id=other, device_id_type=MESH)
+
         compute(4, 1)
+
+        @pl.when(core == 1)
+        def _():
+            pl.semaphore_wait(turn_sem, 1)
+            own(5).start()
+            issue_fwd(5)
+
         compute(4, 0)
-
-        fwd(3).wait_send()
-        own(4).wait_send()
+        chunk_in(5)
+        compute(5, 1, 0, HALF)
+        compute(5, 1, HALF, HALF)
+        compute(5, 0)
+
+        for k in range(2):
+            result_part(N - 1, k * HALF, HALF).wait_send()
         fwd(4).wait_send()
+
+        @pl.when(core == 1)
+        def _():
+            own(5).wait_send()
+
+        fwd(5).wait_send()
         for p in range(2):
             for way in range(2):
                 ring(p, way).wait_send()
@@ -311,7 +379,8 @@
             for turn in range(YLEN):
                 swap(p, turn).wait_send()
         for c in range(N):
-            result(c, pos).wait_send()
+            if c < N - 1:
+                result(c).wait_send()
             pltpu.make_async_copy(mine[c], columns(out_ref, c), l_out.at[c]).wait()
 
 
@@ -331,28 +400,29 @@
         pltpu.SMEM((8, ROW), jnp.int32),
     ]
     scratch += [dma((N,))] * 10
-    scratch += [dma((2, 2))] * 4 + [dma((2, YLEN))] * 2 + [dma] * 5 + [dma((2,))]
+    scratch += [dma((2, 2))] * 4 + [dma((2, YLEN))] * 2 + [dma] * 5 + [dma((2,)), pltpu.SemaphoreType.REGULAR]
+    scratch += [pltpu.VMEM((1, SLOTS), jnp.int32)] * 2 + [dma((2,))] * 3
+    in_hbm = functools.partial(pltpu.with_memory_space_constraint, memory_space=pltpu.HBM)
     any_space = pl.BlockSpec(memory_space=pl.ANY)
-    vmem = pl.BlockSpec(memory_space=pltpu.VMEM)
     smem = pl.BlockSpec(memory_space=pltpu.SMEM)
     result = pl.pallas_call(
         kernel,
         name="ladder",
-        out_shape=jax.ShapeDtypeStruct((BLOCKS, TILE, pair_count), bf16),
-        in_specs=[any_space, any_space, vmem, vmem, smem],
+        out_shape=pltpu.VMEM((BLOCKS, TILE, pair_count), bf16),
+        in_specs=[any_space] * 4 + [smem],
         out_specs=any_space,
         scratch_shapes=scratch,
         compiler_params=pltpu.CompilerParams(
-            collective_id=0, has_side_effects=True, vmem_limit_bytes=60 * 2**20
+            collective_id=0, has_side_effects=True, vmem_limit_bytes=46 * 2**20
         ),
         cost_estimate=pl.CostEstimate(
             flops=4 * SLOTS * TILE * TILE * pair_count, bytes_accessed=8 * 2**20, transcendentals=0
         ),
     )(
-        amplitudes.reshape(BLOCKS, TILE, pair_count),
-        integrals,
-        task_block.reshape(1, SLOTS),
-        task_source.reshape(1, SLOTS),
+        in_hbm(amplitudes.reshape(BLOCKS, TILE, pair_count)),
+        in_hbm(integrals),
+        in_hbm(task_block.reshape(1, SLOTS)),
+        in_hbm(task_source.reshape(1, SLOTS)),
         task_count,
     )
     return result.reshape(BLOCKS * TILE, pair_count)

time: 169 us -> 155 us (0.917)
  Pallas kernels: 164 us -> 152 us
  local copies, waits for them, and re-layouts: 3.76 us -> 1.67 us
    pallas_call x1, Pallas kernels: 164 us -> 152 us  [local(): pl.pallas_call(kernel, name='ladder', out_shape=pltpu.VMEM((BLOCKS, TILE,...]
    unnamed x1, local copies, waits for them, and re-layouts: 3.76 us -> 1.67 us
where the time goes in v2:
time: 155 us
  Pallas kernels  152 us (98%)
  local copies, waits for them, and re-layouts  1.67 us (1%)
    pallas_call x1, Pallas kernels, local(): pl.pallas_call(kernel, name='ladder', out_shape=pltpu.VMEM((BLOCKS, TILE,...  152 us

profile of v2, /device:TPU:1, one launch (start us, length us, event | category | flops | bytes accessed | tf_op | source)
XLA Modules:
  0.0 154.8 jit_solution(7982117640532920115)
XLA Ops:
  0.7 152.4 %ladder.1 = bf16[16,128,768]{2,1,0:T(8,128)(2,1)S(1)} custom-call(bf16[16,128,768]{2,1,0:T(8,128)(2,1)} %bitcast.5, bf16[32,128,128]{2,1,0:T(8,128)(2,1)} %int_ref.1, s32[1,256]{1,0:T(1,128)} %bitcast.6, s32[1,256]{1,0:T(1,128)} %bitcast.7, s32[1]{0:T(128)S(6)} %copy.8.count_ref), custom_call_target="tpu_custom_call" | custom-call | flops 12884901888 | bytes 8388608 | tf_op jit(solution)/shard_map/ladder/pallas_call | solution.py:408
  153.1 1.7 %copy.7 = bf16[2048,768]{1,0:T(8,128)(2,1)} copy(bf16[2048,768]{1,0:T(8,128)(2,1)S(1)} %bitcast.4) | data formatting | bytes 6291456

commit v3 on v2

--- a/solution.py
+++ b/solution.py
@@ -22,7 +22,7 @@
 STARTS = (0, 128, 256, 384, 512, 640)
 N = len(WIDTHS)
 UNROLL = 17
-UNROLL_LAST = 34
+UNROLL_LAST = 68
 
 
 def task_table(count, block, source):
@@ -276,7 +276,7 @@
                 target[b, top : top + rows] = (value * smem[4, b].astype(jnp.float32)).astype(jnp.bfloat16)
                 return carry
 
-            lax.fori_loop(0, BLOCKS, place, 0)
+            lax.fori_loop(0, BLOCKS, place, 0, unroll=BLOCKS)
             if p and rows < TILE:
                 result_part(c, top, rows).start()
             elif p:
@@ -331,27 +331,27 @@
         compute(2, 0)
         fwd(3).wait_send()
 
-        @pl.when(core == 0)
+        @pl.when(core == 1)
         def _():
             own(5).start()
 
         compute(3, 0)
         own(4).wait_send()
 
-        @pl.when(core == 0)
+        @pl.when(core == 1)
         def _():
             issue_fwd(5)
 
         chunk_in(4)
 
-        @pl.when(core == 0)
+        @pl.when(core == 1)
         def _():
             own(5).wait_send()
             pl.semaphore_signal(turn_sem, inc=1, device_id=other, device_id_type=MESH)
 
         compute(4, 1)
 
-        @pl.when(core == 1)
+        @pl.when(core == 0)
         def _():
             pl.semaphore_wait(turn_sem, 1)
             own(5).start()
@@ -367,7 +367,7 @@
             result_part(N - 1, k * HALF, HALF).wait_send()
         fwd(4).wait_send()
 
-        @pl.when(core == 1)
+        @pl.when(core == 0)
         def _():
             own(5).wait_send()
 

time: 155 us -> 154 us (level)
  the two profiles are of different devices: /device:TPU:1 before, /device:TPU:4 now
where the time goes in v3:
time: 154 us
  Pallas kernels  152 us (99%)
  local copies, waits for them, and re-layouts  1.67 us (1%)
    pallas_call x1, Pallas kernels, local(): pl.pallas_call(kernel, name='ladder', out_shape=pltpu.VMEM((BLOCKS, TILE,...  152 us

profile of v3, /device:TPU:4, one launch (start us, length us, event | category | flops | bytes accessed | tf_op | source)
XLA Modules:
  0.0 154.3 jit_solution(16522719289640905429)
XLA Ops:
  0.7 152.0 %ladder.1 = bf16[16,128,768]{2,1,0:T(8,128)(2,1)S(1)} custom-call(bf16[16,128,768]{2,1,0:T(8,128)(2,1)} %bitcast.5, bf16[32,128,128]{2,1,0:T(8,128)(2,1)} %int_ref.1, s32[1,256]{1,0:T(1,128)} %bitcast.6, s32[1,256]{1,0:T(1,128)} %bitcast.7, s32[1]{0:T(128)S(6)} %copy.8.count_ref), custom_call_target="tpu_custom_call" | custom-call | flops 12884901888 | bytes 8388608 | tf_op jit(solution)/shard_map/ladder/pallas_call | solution.py:408
  152.7 1.7 %copy.7 = bf16[2048,768]{1,0:T(8,128)(2,1)} copy(bf16[2048,768]{1,0:T(8,128)(2,1)S(1)} %bitcast.4) | data formatting | bytes 6291456
